TPU v7x, 32 devices: a whole 2x2x4 slice. The times are simulated.
32 devices in a mesh: groups: 2 (over y), scan: 4 (over z), mode: 2 (over x), sub: 2 (over core).
Axes of the slice: x: 2, y: 2, z: 4, core: 2. Of those that a mesh axis runs over, the one named last changes fastest.
Arguments:
- object_field: float32 [2, 2048, 1024], P(None, ('groups', 'scan')), parts along dimension 1, may hold values from -6 to 6
- probe: float32 [8, 2, 256, 256], P('mode', None, 'sub'), may hold values from -3 to 3
- offsets: int32 [8, 4, 2], P(('groups', 'scan')), parts along dimension 0, may hold values from 0 to 768, as said below
- counts: int32 [8], P(('groups', 'scan')), parts along dimension 0, may hold values from 1 to 4, as said below
- measured: float32 [8, 4, 256, 256], P(('groups', 'scan'), None, None, 'sub'), parts along dimension 0, may hold values from 0.25 to 16
Outputs:
- object_grad: float32 [2, 2048, 1024], P(None, ('groups', 'scan'), ('mode', 'sub')), parts along dimension 1
- probe_grad: float32 [16, 2, 256, 256], P(('groups', 'mode'), None, 'sub'), parts along dimension 0
There are 2 independent parts, one for each index of `groups`. A program takes and returns all parts, laid end to end along the dimension named above; an argument that names none is the same for every part. Nothing has to cross between parts.
Inputs may be any that keep to these rules, and one draw needn't show every extreme that they name: Every slot's row offset on tile t lies between t * 256 and t * 256 + 128, and is exactly t * 256 on the last tile; column offsets lie between 0 and 768; some slot reaches each end of both ranges; slots that are not live hold valid offsets too. `counts`: some tile has all 4 slots live.
All inputs are finite; a program needn't handle non-finite values.
Results may differ from a plain program's by a relative error of at most 0.0001.
Values sent between devices are 32-bit elements; how exact they have to be, the bound alone decides.
A program may use at most 64 MiB of HBM per device.

v0:
```python
import math

import jax
import jax.numpy as jnp
from jax import lax
from jax.sharding import PartitionSpec as P

HALO = 128


def shifted(array, axis, by):
    devices = lax.axis_size(axis)
    pairs = [(i, i + by) for i in range(devices) if 0 <= i + by < devices]
    return lax.ppermute(array, axis, pairs)


def transform_tables(length, sign):
    index_row = jnp.arange(length, dtype=jnp.int32)
    products = index_row[:, None] * index_row[None, :] % length
    angles = products.astype(jnp.float32) * (2.0 * math.pi / length)
    cosine = jnp.cos(angles) / math.sqrt(length)
    sine = -sign * jnp.sin(angles) / math.sqrt(length)
    return jnp.stack([jnp.stack([cosine, sine]), jnp.stack([-sine, cosine])])


def regroup(spectra):
    return lax.all_to_all(spectra, "sub", split_axis=4, concat_axis=3, tiled=True)


def local(object_field, probe, offsets, counts, measured):
    tile_index = lax.axis_index("scan")
    sub_index = lax.axis_index("sub")
    tile_rows = object_field.shape[1]
    frame_size = probe.shape[3]
    next_rows = shifted(object_field[:, :HALO], "scan", -1)
    extended = jnp.concatenate([object_field, next_rows], axis=1)
    slot_count = offsets.shape[1]
    slot_offsets = offsets[0]
    measured_frames = measured[0]
    cut_rows = probe.shape[2]
    row_shift = sub_index * cut_rows
    row_starts = slot_offsets[:, 0] - tile_index * tile_rows + row_shift
    col_starts = slot_offsets[:, 1]

    def cut_patch(row_start, col_start):
        return lax.dynamic_slice(
            extended, (jnp.int32(0), row_start, col_start), (2, cut_rows, frame_size)
        )

    patches = jax.vmap(cut_patch)(row_starts, col_starts)
    live_slot = (jnp.arange(slot_count, dtype=jnp.int32) < counts[0]).astype(jnp.float32)
    probe_re = probe[:, 0][:, None]
    probe_im = probe[:, 1][:, None]
    patch_re = patches[:, 0][None]
    patch_im = patches[:, 1][None]
    exit_wave = jnp.stack(
        [probe_re * patch_re - probe_im * patch_im, probe_re * patch_im + probe_im * patch_re],
        axis=2,
    )
    forward_table = transform_tables(frame_size, 1.0)
    inverse_table = transform_tables(frame_size, -1.0)
    highest = lax.Precision.HIGHEST
    column_pass = jnp.einsum("mcarx,abxy->mcbry", exit_wave, forward_table, precision=highest)
    column_pass = regroup(column_pass)
    spectra = jnp.einsum("abjr,mcarx->mcbjx", forward_table, column_pass, precision=highest)
    energy = jnp.sum(spectra * spectra, axis=(0, 2))
    intensity = lax.psum(energy, "mode")
    scaling = live_slot[:, None, None] * (
        1.0 - jnp.sqrt(measured_frames + 1.0) / jnp.sqrt(intensity + 1.0)
    )
    weighted = spectra * scaling[None, :, None]
    row_back = jnp.einsum("abrj,mcajx->mcbxr", inverse_table, weighted, precision=highest)
    row_back = regroup(row_back)
    chi_field = jnp.einsum("mcaxr,abxy->mcbry", row_back, inverse_table, precision=highest)
    chi_re = chi_field[:, :, 0]
    chi_im = chi_field[:, :, 1]
    object_terms = jnp.stack(
        [
            jnp.sum(probe_re * chi_re + probe_im * chi_im, axis=0),
            jnp.sum(probe_re * chi_im - probe_im * chi_re, axis=0),
        ],
        axis=1,
    )
    probe_terms = jnp.stack(
        [
            jnp.sum(patch_re * chi_re + patch_im * chi_im, axis=1),
            jnp.sum(patch_re * chi_im - patch_im * chi_re, axis=1),
        ],
        axis=1,
    )
    probe_grad = lax.psum(probe_terms, "scan") / lax.axis_size("scan")

    def add_slot(slot_index, buffer):
        start_row = row_starts[slot_index]
        start_col = col_starts[slot_index]
        current = lax.dynamic_slice(
            buffer, (jnp.int32(0), start_row, start_col), (2, cut_rows, frame_size)
        )
        return lax.dynamic_update_slice(
            buffer, current + object_terms[slot_index], (jnp.int32(0), start_row, start_col)
        )

    buffer = jnp.zeros((2, tile_rows + HALO, object_field.shape[2]), jnp.float32)
    buffer = lax.fori_loop(0, slot_count, add_slot, buffer)
    arrived = shifted(buffer[:, tile_rows:], "scan", 1)
    own_rows = buffer[:, :tile_rows].at[:, :HALO].add(arrived)
    object_grad = lax.psum_scatter(own_rows, ("mode", "sub"), scatter_dimension=2, tiled=True)
    return (object_grad, probe_grad)


def solution(mesh):
    in_specs = (
        P(None, ("groups", "scan"), None),
        P("mode", None, "sub", None),
        P(("groups", "scan"), None, None),
        P(("groups", "scan")),
        P(("groups", "scan"), None, None, "sub"),
    )
    out_specs = (
        P(None, ("groups", "scan"), ("mode", "sub")),
        P(("groups", "mode"), None, "sub", None),
    )
    return jax.shard_map(local, mesh=mesh, in_specs=in_specs, out_specs=out_specs, check_vma=False)
```

profile of v0, /device:TPU:24, one launch (start us, length us, event | category | flops | bytes accessed | tf_op | source)
XLA Modules:
  0.0 323.6 jit_solution(17357555192799736739)
XLA Ops:
  7.2 1.3 slice.61
  8.5 3.3 %collective-permute-start = (f32[2,128,1024]{2,1,0:T(8,128)S(1)}, f32[2,128,1024]{2,1,0:T(8,128)}, u32[]{:S(2)}, u32[]{:S(2)}) collective-permute-start(f32[2,128,1024]{2,1,0:T(8,128)S(1)} %slice.61), channel_id=1, source_target_pairs={{4,0},{8,4},{12,8},{5,1},{9,5},{13,9},{6,2},{10,6},{14,10},{7,3},{... | collective-permute-start | bytes 3145736 | tf_op jit(solution)/shard_map/ppermute | solution.py:14
  13.7 1.1 cosine_multiply_fusion
  15.8 1.4 fusion.18
  17.2 16.1 %collective-permute-done = f32[2,128,1024]{2,1,0:T(8,128)} collective-permute-done((f32[2,128,1024]{2,1,0:T(8,128)S(1)}, f32[2,128,1024]{2,1,0:T(8,128)}, u32[]{:S(2)}, u32[]{:S(2)}) %collective-permute-start) | collective-permute-done | bytes 1048608 | tf_op jit(solution)/shard_map/ppermute | solution.py:14
  33.3 1.6 pad_maximum_fusion
  34.9 11.3 %while.16 = (s32[]{:T(128)}, f32[2,384,1024]{2,1,0:T(8,128)S(1)}, s32[4,3]{1,0:T(4,128)S(1)}, f32[4,2,128,256]{3,2,1,0:T(8,128)}, s32[]{:T(128)}) while((s32[]{:T(128)}, f32[2,384,1024]{2,1,0:T(8,128)S(1)}, s32[4,3]{1,0:T(4,128)S(1)}, f32[4,2,128,256]{3,2,1,0:T(8,128)}, s32[]{:T(128)}) %tuple.73), condition=%wide.while_cond.1, body=%wide.while_body.1.sunk | while | flops 2 | bytes 525929 | solution.py:46
  35.8 2.1 bitcast_dynamic-update-slice_fusion.2
  38.5 2.1 bitcast_dynamic-update-slice_fusion.2
  41.3 2.1 bitcast_dynamic-update-slice_fusion.2
  44.1 2.1 bitcast_dynamic-update-slice_fusion.2
  46.2 1.7 slice_bitcast_fusion.4
  49.1 7.1 %fusion.8 = f32[4,4,2,128,256]{3,4,1,0,2:T(8,128)S(1)} fusion(f32[4,4,1,128,256]{4,3,2,1,0:T(8,128)S(1)} %get-tuple-element.161, f32[4,4,1,128,256]{4,3,2,1,0:T(8,128)S(1)} %get-tuple-element.160, f32[1,2,256,256]{2,3,0,1:T(8,128)S(1)} %copy-done.4, f32[1,2,256,256]{2,3,0,1:T(8,128)S(1)} %copy-done.5), kind=kOutput, calls=%fused_computation.17 | convolution fusion | flops 6443761664 | bytes 9437184 | tf_op jit(solution)/shard_map/mcarx,abxy->mcbry/dot_general | solution.py:63
  56.3 2.7 copy.22
  59.0 7.1 %all_to_all.36 = f32[4,4,2,128,256]{3,1,0,2,4:T(4,128)S(1)} all-to-all(f32[4,4,2,128,256]{3,1,0,2,4:T(4,128)S(1)} %copy.22), channel_id=1, replica_groups=mesh['groups'=2,'scan'=4,'mode'=2,'sub'=2] {'sub'}, dimensions={4} | all-to-all | bytes 8388608 | tf_op jit(solution)/shard_map/all_to_all | solution.py:27
  66.1 5.2 %copy.54 = f32[4,4,2,128,2,128]{3,4,5,2,1,0:T(2,128)} copy(f32[4,4,2,128,2,128]{3,1,0,2,5,4:T(4,128)S(1)} %bitcast.153) | data formatting | bytes 8388608 | tf_op jit(solution)/shard_map/all_to_all | solution.py:27
  71.2 6.5 %reshape.199 = f32[4,4,2,256,128,1]{3,4,2,1,0,5:T(8,128)} reshape(f32[4,4,2,2,128,128]{4,3,5,2,1,0:T(2,128)} %bitcast.154) | data formatting | bytes 8388608 | tf_op jit(solution)/shard_map/all_to_all | solution.py:27
  77.7 10.8 %fusion.5 = (f32[4,256,128]{1,2,0:T(8,128)}, f32[4,4,128,2,256,1]{4,2,5,3,1,0:T(8,128)}) fusion(f32[1,2,256,256]{2,3,0,1:T(8,128)S(1)} %copy-done.4, f32[1,2,256,256]{2,3,0,1:T(8,128)S(1)} %copy-done.5, f32[4,4,2,256,128,1]{3,4,2,1,0,5:T(8,128)} %reshape.199), kind=kOutput, calls=%fused_computation.12 | convolution fusion | flops 6444679168 | bytes 9961472 | tf_op jit(solution)/shard_map/abjr,mcarx->mcbjx/dot_general | solution.py:65
  88.5 2.1 copy.25
  91.3 1.0 copy.19
  93.0 26.4 %all-reduce.3.cloned.1.call-done = f32[4,256,128]{1,2,0:T(8,128)} async-done(((f32[4,256,128]{1,2,0:T(8,128)}), f32[4,256,128]{1,2,0:T(8,128)}) %all-reduce.3.cloned.1.call-update) | async-done | bytes 524304 | tf_op jit(solution)/shard_map/psum | solution.py:67
  119.3 1.4 fusion.21
  120.8 10.0 %fusion.9 = f32[4,4,2,128,256]{4,3,2,1,0:T(8,128)} fusion(f32[4,4,128,2,256,1]{4,2,5,3,1,0:T(8,128)} %get-tuple-element.175, f32[4,256,128]{1,2,0:T(8,128)S(1)} %fusion.21, f32[1,2,256,256]{2,3,1,0:T(8,128)S(1)} %copy-done.3, f32[1,2,256,256]{2,3,1,0:T(8,128)S(1)} %copy-done.2), kind=kOutput, calls=%fused_computation.18 | convolution fusion | flops 6443761664 | bytes 9961472 | tf_op jit(solution)/shard_map/abrj,mcajx->mcbxr/dot_general | solution.py:72
  130.8 7.3 %copy.27 = f32[4,4,2,128,256]{3,2,1,0,4:T(2,128)} copy(f32[4,4,2,128,256]{4,3,2,1,0:T(8,128)} %fusion.9) | data formatting | bytes 8388608 | tf_op jit(solution)/shard_map/abrj,mcajx->mcbxr/transpose | solution.py:72
  138.1 11.9 %all_to_all.37 = f32[4,4,2,128,256]{3,2,1,0,4:T(2,128)} all-to-all(f32[4,4,2,128,256]{3,2,1,0,4:T(2,128)} %copy.27), channel_id=1, replica_groups=mesh['groups'=2,'scan'=4,'mode'=2,'sub'=2] {'sub'}, dimensions={4} | all-to-all | bytes 8388608 | tf_op jit(solution)/shard_map/all_to_all | solution.py:27
  149.9 7.4 %copy.28 = f32[4,4,2,128,2,128]{5,3,4,2,1,0:T(8,128)} copy(f32[4,4,2,128,2,128]{3,2,1,0,5,4:T(2,128)} %bitcast.155) | data formatting | bytes 8388608 | tf_op jit(solution)/shard_map/all_to_all | solution.py:27
  157.3 8.8 %convolution_bitcast_fusion = f32[4,4,2,128,256]{3,4,1,0,2:T(8,128)S(1)} fusion(f32[4,4,2,256,128,1]{4,3,2,1,0,5:T(8,128)} %bitcast.152, f32[1,2,256,256]{2,3,1,0:T(8,128)S(1)} %copy-done.3, f32[1,2,256,256]{2,3,1,0:T(8,128)S(1)} %copy-done.2), kind=kOutput, calls=%fused_computation.19 | convolution fusion | flops 6442713088 | bytes 9437184 | tf_op jit(solution)/shard_map/mcaxr,abxy->mcbry/dot_general | solution.py:74
  166.2 2.1 add_reduce_fusion
  168.3 2.0 broadcast_in_dim.2
  170.3 41.7 %while.15 = (s32[]{:T(128)}, f32[2,384,1024]{2,1,0:T(8,128)}, s32[4]{0:T(128)S(1)}, s32[4]{0:T(128)S(1)}, f32[4,2,128,256]{2,3,0,1:T(8,128)S(1)}, /*index=5*/s32[]{:T(128)}, s32[]{:T(128)}, s32[]{:T(128)}, s32[]{:T(128)}) while((s32[]{:T(128)}, f32[2,384,1024]{2,1,0:T(8,128)}, s32[4]{0:T(128)S(1)}, s32[4]{0:T(128)S(1)}, ...), condition=%wide.region_5.6_spmd, body=%wide.region_4.5_spmd.sunk | while | flops 65544 | bytes 2359497 | solution.py:104
  175.6 1.2 bitcast_add_fusion.2
  176.7 4.0 %dynamic_update_slice.8 = f32[2,384,1024]{2,1,0:T(8,128)} dynamic-update-slice(f32[2,384,1024]{2,1,0:T(8,128)} %get-tuple-element.267, f32[2,128,256]{2,1,0:T(8,128)S(1)} %bitcast_add_fusion.2, s32[]{:T(128)} %constant.99.clone.1..sunk, s32[]{:T(128)S(6)} %select_n.101, s32[]{:T(128)S(6)} %select_n.102) | dynamic-update-slice | bytes 524292 | tf_op jit(solution)/shard_map/while/body/eval_jaxpr/dynamic_update_slice | solution.py:99
  186.0 1.2 bitcast_add_fusion.2
  187.2 4.0 %dynamic_update_slice.8 = f32[2,384,1024]{2,1,0:T(8,128)} dynamic-update-slice(f32[2,384,1024]{2,1,0:T(8,128)} %get-tuple-element.267, f32[2,128,256]{2,1,0:T(8,128)S(1)} %bitcast_add_fusion.2, s32[]{:T(128)} %constant.99.clone.1..sunk, s32[]{:T(128)S(6)} %select_n.101, s32[]{:T(128)S(6)} %select_n.102) | dynamic-update-slice | bytes 524292 | tf_op jit(solution)/shard_map/while/body/eval_jaxpr/dynamic_update_slice | solution.py:99
  196.4 1.2 bitcast_add_fusion.2
  197.6 4.0 %dynamic_update_slice.8 = f32[2,384,1024]{2,1,0:T(8,128)} dynamic-update-slice(f32[2,384,1024]{2,1,0:T(8,128)} %get-tuple-element.267, f32[2,128,256]{2,1,0:T(8,128)S(1)} %bitcast_add_fusion.2, s32[]{:T(128)} %constant.99.clone.1..sunk, s32[]{:T(128)S(6)} %select_n.101, s32[]{:T(128)S(6)} %select_n.102) | dynamic-update-slice | bytes 524292 | tf_op jit(solution)/shard_map/while/body/eval_jaxpr/dynamic_update_slice | solution.py:99
  206.8 1.2 bitcast_add_fusion.2
  208.0 4.1 %dynamic_update_slice.8 = f32[2,384,1024]{2,1,0:T(8,128)} dynamic-update-slice(f32[2,384,1024]{2,1,0:T(8,128)} %get-tuple-element.267, f32[2,128,256]{2,1,0:T(8,128)S(1)} %bitcast_add_fusion.2, s32[]{:T(128)} %constant.99.clone.1..sunk, s32[]{:T(128)S(6)} %select_n.101, s32[]{:T(128)S(6)} %select_n.102) | dynamic-update-slice | bytes 524292 | tf_op jit(solution)/shard_map/while/body/eval_jaxpr/dynamic_update_slice | solution.py:99
  212.1 2.5 slice.69
  214.5 1.3 collective-permute-start.1
  215.8 2.3 pad_maximum_fusion.3
  218.1 1.5 slice.67
  219.6 39.3 %collective-permute-done.1 = f32[2,128,1024]{2,1,0:T(8,128)} collective-permute-done((f32[2,128,1024]{2,1,0:T(8,128)}, f32[2,128,1024]{2,1,0:T(8,128)}, u32[]{:S(2)}, u32[]{:S(2)}) %collective-permute-start.1) | collective-permute-done | bytes 1048608 | tf_op jit(solution)/shard_map/ppermute | solution.py:14
  259.0 2.3 add_dynamic-update-slice_fusion
  261.3 20.3 %all-reduce.5.cloned.1.call-done = f32[4,2,128,256]{2,3,0,1:T(8,128)} async-done(((f32[4,2,128,256]{2,3,0,1:T(8,128)}), f32[4,2,128,256]{2,3,0,1:T(8,128)}) %all-reduce.5.cloned.1.call-update) | async-done | bytes 1048592 | tf_op jit(solution)/shard_map/psum | solution.py:91
  281.7 1.3 broadcast_multiply_fusion
  283.0 1.3 copy.34
  284.3 32.8 %reduce-scatter.2.cloned.1.call-done = f32[2,256,256]{2,1,0:T(8,128)} async-done(((f32[2,256,1024]{2,1,0:T(8,128)}), f32[2,256,256]{2,1,0:T(8,128)}) %reduce-scatter.2.cloned.1.call-update) | async-done | bytes 524304 | tf_op jit(solution)/shard_map/reduce_scatter | solution.py:107
  (57 shorter events, 12.8 us)
Async XLA Ops:
  7.2 112.2 %all-reduce.3.cloned.1.call-start = ((), (), s32[]{:S(2)}) async-start(), calls=%async_computation.3 | async-start | bytes 1048576 | tf_op jit(solution)/shard_map/psum | solution.py:67
  8.5 24.8 %collective-permute-start = (f32[2,128,1024]{2,1,0:T(8,128)S(1)}, f32[2,128,1024]{2,1,0:T(8,128)}, u32[]{:S(2)}, u32[]{:S(2)}) collective-permute-start(f32[2,128,1024]{2,1,0:T(8,128)S(1)} %slice.61), channel_id=1, source_target_pairs={{4,0},{8,4},{12,8},{5,1},{9,5},{13,9},{6,2},{10,6},{14,10},{7,3},{... | collective-permute-start | bytes 3145736 | tf_op jit(solution)/shard_map/ppermute | solution.py:14
  12.7 20.6 %copy-start.1 = (f32[2,256,1024]{2,1,0:T(8,128)S(1)}, f32[2,256,1024]{2,1,0:T(8,128)}, u32[]{:S(2)}) copy-start(f32[2,256,1024]{2,1,0:T(8,128)} %param.9) | copy-start | bytes 6291460
  47.9 1.0 copy-start.4
  47.9 1.2 copy-start.5
  88.5 193.2 %all-reduce.5.cloned.1.call-start = ((), (), s32[]{:S(2)}) async-start(), calls=%async_computation.5 | async-start | bytes 2097152 | tf_op jit(solution)/shard_map/psum | solution.py:91
  90.6 30.2 %copy-start.2 = (f32[1,2,256,256]{2,3,1,0:T(8,128)S(1)}, f32[1,2,256,256]{2,3,1,0:T(8,128)}, u32[]{:S(2)}) copy-start(f32[1,2,256,256]{2,3,1,0:T(8,128)} %get-tuple-element.166) | copy-start | bytes 1572868
  90.6 30.2 %copy-start.3 = (f32[1,2,256,256]{2,3,1,0:T(8,128)S(1)}, f32[1,2,256,256]{2,3,1,0:T(8,128)}, u32[]{:S(2)}) copy-start(f32[1,2,256,256]{2,3,1,0:T(8,128)} %get-tuple-element.169) | copy-start | bytes 1572868
  157.3 8.9 %copy-start.6 = (f32[4,128,256]{1,2,0:T(8,128)S(1)}, f32[4,128,256]{1,2,0:T(8,128)}, u32[]{:S(2)}) copy-start(f32[4,128,256]{1,2,0:T(8,128)} %copy.19) | copy-start | bytes 1572868
  212.1 6.1 %copy-start = (f32[2,384,1024]{2,1,0:T(8,128)S(1)}, f32[2,384,1024]{2,1,0:T(8,128)}, u32[]{:S(2)}) copy-start(f32[2,384,1024]{2,1,0:T(8,128)} %get-tuple-element.108) | copy-start | bytes 9437188
  214.5 44.4 %collective-permute-start.1 = (f32[2,128,1024]{2,1,0:T(8,128)}, f32[2,128,1024]{2,1,0:T(8,128)}, u32[]{:S(2)}, u32[]{:S(2)}) collective-permute-start(f32[2,128,1024]{2,1,0:T(8,128)} %slice.69), channel_id=1, source_target_pairs={{0,4},{4,8},{8,12},{1,5},{5,9},{9,13},{2,6},{6,10},{10,14},{3,7},{... | collective-permute-start | bytes 3145736 | tf_op jit(solution)/shard_map/ppermute | solution.py:14
  218.1 99.0 %reduce-scatter.2.cloned.1.call-start = ((), (), s32[]{:S(2)}) async-start(), calls=%async_computation.4 | async-start | bytes 2621440 | tf_op jit(solution)/shard_map/reduce_scatter | solution.py:107
Sparse Core Ops, SparseCore 0:
  88.6 30.6 all-reduce.2
  218.2 63.4 all-reduce.4
  284.8 32.3 reduce-scatter.1
where the time goes:
time: 327 us; the launch traced here: 324 us
  waiting for transfers between devices  135 us (41%)
  local copies, waits for them, and re-layouts  76.2 us (23%)
  matrix products  36.8 us (11%)
  other arithmetic  21.5 us (7%)
  blocking collectives  19 us (6%)
  loops' own time  15.8 us (5%)
  between operations  14.7 us (4%)
  starting transfers between devices  4.74 us (1%)
    ppermute x2, waiting for transfers between devices, shifted(): return lax.ppermute(array, axis, pairs)  55.4 us
    reduce_scatter x1, waiting for transfers between devices, local(): lax.psum_scatter(own_rows, ('mode', 'sub'), scatter_dimension=2, tiled=True)  32.8 us
    psum x1, waiting for transfers between devices, local(): intensity = lax.psum(energy, 'mode')  26.4 us
    psum x1, waiting for transfers between devices, local(): probe_grad = lax.psum(probe_terms, 'scan') / lax.axis_size('scan')  20.3 us
    all_to_all x3, local copies, waits for them, and re-layouts, regroup(): lax.all_to_all(spectra, 'sub', split_axis=4, concat_axis=3, tiled=True)  19 us
    all_to_all x2, blocking collectives, regroup(): lax.all_to_all(spectra, 'sub', split_axis=4, concat_axis=3, tiled=True)  19 us
    dynamic_update_slice x4, local copies, waits for them, and re-layouts, add_slot(): lax.dynamic_update_slice(buffer, current + object_terms[slot_index], (jnp...  16.1 us
    another operation x1, loops' own time, local(): buffer = lax.fori_loop(0, slot_count, add_slot, buffer)  15.6 us
  transfers between devices with their start and end apart: 5, of which 5 were waited for; matrix products, arithmetic and copies ran while one was open for 5% of the time, Pallas kernels for 0%

commit v1 on v0

v1 whole, which is shorter than its diff:
```python
import functools
import math

import jax
import jax.numpy as jnp
import numpy as np
from jax import lax
from jax.experimental import pallas as pl
from jax.experimental.pallas import tpu as pltpu
from jax.sharding import PartitionSpec as P

HALO = 128
MESH = pl.DeviceIdType.MESH


def split_table(table):
    high = table.astype(np.float32).astype(jnp.bfloat16)
    low = (table - high.astype(np.float64)).astype(np.float32).astype(jnp.bfloat16)
    return high, low


def transform_tables(length):
    index = np.arange(length)
    angles = (index[:, None] * index[None, :] % length) * (2.0 * math.pi / length)
    cosine = np.cos(angles) / math.sqrt(length)
    sine = np.sin(angles) / math.sqrt(length)
    parts = []
    for table in (cosine, cosine + sine, cosine - sine):
        parts.extend(split_table(table))
    return np.stack(parts)


def split(x):
    high = x.astype(jnp.bfloat16)
    low = (x - high.astype(jnp.float32)).astype(jnp.bfloat16)
    return high, low


def mm(a, b):
    return jnp.dot(a, b, preferred_element_type=jnp.float32)


def mm_t(a, b):
    return lax.dot_general(a, b, (((1,), (1,)), ((), ())), preferred_element_type=jnp.float32)


def dot3(a, b):
    return mm(a[0], b[0]) + (mm(a[1], b[0]) + mm(a[0], b[1]))


def selectors(offsets, counts, tile_start, first, slots, frame, tile, obj_c):
    own = lax.dynamic_slice_in_dim(offsets[0], first, slots, axis=0)
    pixel = jnp.arange(frame, dtype=jnp.int32)
    row = (own[:, :1] - tile_start) + pixel
    col = (own[:, 1:] + pixel).reshape(1, slots * frame)
    rows = jnp.arange(tile + HALO, dtype=jnp.int32)
    cols = jnp.arange(obj_c, dtype=jnp.int32)[:, None]
    take_rows = (row[:, :, None] == rows[None, None, :]).astype(jnp.bfloat16)
    put_rows = (rows[None, :, None] == row[:, None, :]).astype(jnp.bfloat16)
    take_cols = (cols == col).astype(jnp.bfloat16)
    live = (first + jnp.arange(slots, dtype=jnp.int32) < counts[0]).astype(jnp.float32)
    return take_rows, put_rows, take_cols, jnp.broadcast_to(live[:, None, None], (slots, 1, frame))


def kernel(
    n, nm, obj, probe, take_rows, put_rows, take_cols, live, meas, tabs, og, pg,
    ext, pf, mf, q, spec, inten, inten_in, objt, pterm, px, x, p_left, p_right, tot,
    g, g_in, h, h_in, hz,
    loc_sem, probe_sem, meas_sem, halo_sem, fwd_sem, int_sem, px_sem, part_send, pl_sem, pr_sem,
    tot_out, tot_in, gs_sem, hs_sem, hz_sem,
):
    t = lax.axis_index("scan")
    mode = lax.axis_index("mode")
    sub = lax.axis_index("sub")
    sib = 1 - sub
    tile = obj.shape[1]
    obj_c = obj.shape[2]
    nk = probe.shape[0]
    cut = probe.shape[2]
    frame = probe.shape[3]
    mcols = meas.shape[3]
    slots = mf.shape[0]
    width = og.shape[2]
    half = obj_c // 2
    chunks = x.shape[0]
    owner = (n - 1) // 2

    def remote(src, dst, send, recv, **where):
        return pltpu.make_async_remote_copy(
            src_ref=src, dst_ref=dst, send_sem=send, recv_sem=recv,
            device_id=where, device_id_type=MESH,
        )

    barrier = pltpu.get_barrier_semaphore()
    pl.semaphore_signal(barrier, inc=1, device_id={"sub": sib}, device_id_type=MESH)
    for d in range(1, nm):
        pl.semaphore_signal(
            barrier, inc=1, device_id={"mode": lax.rem(mode + d, nm)}, device_id_type=MESH
        )

    @pl.when(t > 0)
    def _():
        pl.semaphore_signal(barrier, inc=1, device_id={"scan": t - 1}, device_id_type=MESH)

    @pl.when(t < n - 1)
    def _():
        pl.semaphore_signal(barrier, inc=1, device_id={"scan": t + 1}, device_id_type=MESH)

    own_obj = pltpu.make_async_copy(obj, ext.at[:, pl.ds(0, tile)], loc_sem.at[0])
    own_rows = pl.ds(pl.multiple_of(sub * cut, cut), cut)
    sib_rows = pl.ds(pl.multiple_of(sib * cut, cut), cut)
    own_probe = pltpu.make_async_copy(probe, pf.at[:, :, own_rows], loc_sem.at[1])
    own_mcols = pl.ds(pl.multiple_of(sub * mcols, mcols), mcols)
    own_meas = pltpu.make_async_copy(
        meas.at[0, pl.ds(sub * slots, slots)], mf.at[:, :, own_mcols], loc_sem.at[2]
    )
    own_obj.start()
    own_probe.start()
    own_meas.start()
    pl.semaphore_wait(
        barrier, nm + (t > 0).astype(jnp.int32) + (t < n - 1).astype(jnp.int32)
    )

    own_half = pl.ds(pl.multiple_of(sub * half, half), half)

    def halo(c):
        return remote(
            obj.at[c, pl.ds(0, HALO), own_half], ext.at[c, pl.ds(tile, HALO), own_half],
            halo_sem.at[0, c], halo_sem.at[1, c], scan=jnp.maximum(t - 1, 0),
        )

    def forwarded(c):
        part = ext.at[c, pl.ds(tile, HALO), own_half]
        return remote(part, part, fwd_sem.at[0, c], fwd_sem.at[1, c], sub=sib)

    @pl.when(t > 0)
    def _():
        halo(0).start()
        halo(1).start()

    send_probe = remote(
        probe, pf.at[:, :, own_rows], probe_sem.at[0], probe_sem.at[1], sub=sib
    )
    send_probe.start()
    send_meas = remote(
        meas.at[0, pl.ds(sib * slots, slots)], mf.at[:, :, own_mcols],
        meas_sem.at[0], meas_sem.at[1], sub=sib,
    )
    send_meas.start()

    objt[...] = jnp.zeros_like(objt)
    inten[...] = jnp.zeros_like(inten)

    @pl.when(t < n - 1)
    def _():
        for c in range(2):
            halo(c).wait_recv()
            forwarded(c).start()
        for c in range(2):
            forwarded(c).wait_send()
            forwarded(c).wait_recv()

    own_obj.wait()

    @pl.when(t == n - 1)
    def _():
        ext[:, pl.ds(tile, HALO)] = jnp.zeros((2, HALO, obj_c), jnp.float32)

    own_probe.wait()
    send_probe.wait()

    for c in range(2):
        high, low = split(ext[c])
        picked = mm(high, take_cols[...]) + mm(low, take_cols[...])
        for s in range(slots):
            high, low = split(picked[:, s * frame : (s + 1) * frame])
            q[s, c] = mm(take_rows[s], high) + mm(take_rows[s], low)

    def table(i):
        return tabs[2 * i], tabs[2 * i + 1]

    def right(re, im, a, b):
        mid = dot3(split(re + im), table(0))
        return mid - dot3(split(im), table(b)), mid - dot3(split(re), table(a))

    def left(re, im, a, b):
        mid = dot3(table(0), split(re + im))
        return mid - dot3(table(b), split(im)), mid - dot3(table(a), split(re))

    def send_inten(s, d):
        return remote(
            inten.at[s], inten_in.at[s, d - 1], int_sem.at[0, s, d - 1],
            int_sem.at[1, s, d - 1], mode=lax.rem(mode + d, nm),
        )

    for s in range(slots):

        def forward(k, carry):
            pr, pi = pf[k, 0], pf[k, 1]
            qr, qi = q[s, 0], q[s, 1]
            yr, yi = right(pr * qr - pi * qi, pr * qi + pi * qr, 1, 2)
            zr, zi = left(yr, yi, 1, 2)
            spec[s, k, 0] = zr
            spec[s, k, 1] = zi
            inten[s] += zr * zr + zi * zi
            return carry

        lax.fori_loop(0, nk, forward, 0)
        for d in range(1, nm):
            send_inten(s, d).start()

    own_meas.wait()
    send_meas.wait()

    def px_copy(k):
        return remote(
            pterm.at[k, :, sib_rows], px.at[k], px_sem.at[0, k], px_sem.at[1, k], sub=sib
        )

    not_owner = t != owner
    has_outer = jnp.logical_and(t > 0, t < n - 1)
    below = t < owner

    def part_right(c):
        return remote(
            x.at[c], p_left.at[c], part_send.at[c], pl_sem.at[c], scan=jnp.minimum(t + 1, n - 1)
        )

    def part_left(c):
        return remote(
            x.at[c], p_right.at[c], part_send.at[c], pr_sem.at[c], scan=jnp.maximum(t - 1, 0)
        )

    def total_left(c):
        return remote(
            tot.at[c], tot.at[c], tot_out.at[0, c], tot_in.at[c], scan=jnp.maximum(t - 1, 0)
        )

    def total_right(c):
        return remote(
            tot.at[c], tot.at[c], tot_out.at[1, c], tot_in.at[c], scan=jnp.minimum(t + 1, n - 1)
        )

    def send_part(c):
        @pl.when(below)
        def _():
            part_right(c).start()

        @pl.when(t > owner)
        def _():
            part_left(c).start()

    def ready(k):
        px_copy(k).wait_recv()
        for c in range(2):
            x[2 * k + c] = pterm[k, c, own_rows] + px[k, c]

        @pl.when(jnp.logical_and(not_owner, jnp.logical_not(has_outer)))
        def _():
            for c in range(2):
                send_part(2 * k + c)

    for s in range(slots):
        for d in range(1, nm):
            send_inten(s, d).wait_recv()
        total = inten[s]
        for d in range(1, nm):
            total = total + inten_in[s, d - 1]
        inten_in[s, 0] = live[s] * (1.0 - jnp.sqrt(mf[s] + 1.0) * lax.rsqrt(total + 1.0))

        def backward(k, carry):
            scale = inten_in[s, 0]
            yr, yi = left(spec[s, k, 0] * scale, spec[s, k, 1] * scale, 2, 1)
            cr, ci = right(yr, yi, 2, 1)
            pr, pi = pf[k, 0], pf[k, 1]
            qr, qi = q[s, 0], q[s, 1]
            objt[s, 0] += pr * cr + pi * ci
            objt[s, 1] += pr * ci - pi * cr
            tr = qr * cr + qi * ci
            ti = qr * ci - qi * cr
            if s == 0:
                pterm[k, 0] = tr
                pterm[k, 1] = ti
            else:
                pterm[k, 0] += tr
                pterm[k, 1] += ti
            if s == slots - 1:
                px_copy(k).start()

                @pl.when(k > 0)
                def _():
                    ready(k - 1)

            return carry

        lax.fori_loop(0, nk, backward, 0)

    ready(nk - 1)

    for c in range(2):
        placed = []
        for s in range(slots):
            high, low = split(objt[s, c])
            placed.append(mm(put_rows[s], high) + mm(put_rows[s], low))
        high, low = split(jnp.concatenate(placed, axis=1))
        g[c] = mm_t(high, take_cols[...]) + mm_t(low, take_cols[...])

    spans = (pl.ds(tile, HALO), pl.ds(0, tile))

    def block(m, s):
        return pl.ds(pl.multiple_of((m * 2 + s) * width, width), width)

    def sib_send(m, e):
        return remote(
            g.at[:, spans[e], block(m, sib)], g_in.at[m, :, spans[e]],
            gs_sem.at[0, m, e], gs_sem.at[1, m, e], sub=sib,
        )

    def mode_send(d, e):
        m = lax.rem(mode + d, nm)
        return remote(
            h.at[m, :, spans[e]], h_in.at[d - 1, :, spans[e]],
            hs_sem.at[0, d - 1, e], hs_sem.at[1, d - 1, e], mode=m,
        )

    edge = remote(
        h.at[mode, :, spans[0]], hz, hz_sem.at[0], hz_sem.at[1], scan=jnp.minimum(t + 1, n - 1)
    )

    def start_sib():
        for e in range(2):
            for m in range(nm):
                sib_send(m, e).start()

    def sum_sib():
        for e in range(2):
            for m in range(nm):
                sib_send(m, e).wait_recv()
                h[m, :, spans[e]] = g[:, spans[e], block(m, sub)] + g_in[m, :, spans[e]]
            for d in range(1, nm):
                mode_send(d, e).start()

    def sum_mode(e):
        for d in range(1, nm):
            mode_send(d, e).wait_recv()
        whole = h[mode, :, spans[e]]
        for d in range(1, nm):
            whole = whole + h_in[d - 1, :, spans[e]]
        if e == 0:
            h[mode, :, spans[e]] = whole

            @pl.when(t < n - 1)
            def _():
                edge.start()
        else:
            og[...] = whole

    def inward(c):
        @pl.when(jnp.logical_and(not_owner, has_outer))
        def _():
            @pl.when(below)
            def _():
                part_right(c).wait_recv()
                x[c] += p_left[c]

            @pl.when(t > owner)
            def _():
                part_left(c).wait_recv()
                x[c] += p_right[c]

            send_part(c)

        @pl.when(t == owner)
        def _():
            if owner > 0:
                part_right(c).wait_recv()
                x[c] += p_left[c]
            if owner < n - 1:
                part_left(c).wait_recv()
                x[c] += p_right[c]
            tot[c] = x[c] * (1.0 / n)
            if owner > 0:
                total_left(c).start()
            if owner < n - 1:
                total_right(c).start()
            pg[c // 2, c % 2] = tot[c]

    def outward(c):
        @pl.when(not_owner)
        def _():
            total_left(c).wait_recv()

            @pl.when(jnp.logical_and(below, t > 0))
            def _():
                total_left(c).start()

            @pl.when(jnp.logical_and(t > owner, t < n - 1))
            def _():
                total_right(c).start()

            pg[c // 2, c % 2] = tot[c]

    start_sib()
    inward(0)
    sum_sib()
    lag = 2
    for c in range(1, chunks + lag):
        if c < chunks:
            inward(c)
        if c >= lag:
            outward(c - lag)
        if c == chunks // 2:
            sum_mode(0)
    sum_mode(1)

    @pl.when(t > 0)
    def _():
        edge.wait_recv()
        og[:, pl.ds(0, HALO)] += hz[...]

    @pl.when(t > 0)
    def _():
        halo(0).wait_send()
        halo(1).wait_send()

    @pl.when(t < n - 1)
    def _():
        edge.wait_send()

    for s in range(slots):
        for d in range(1, nm):
            send_inten(s, d).wait_send()
    for k in range(nk):
        px_copy(k).wait_send()
    for e in range(2):
        for m in range(nm):
            sib_send(m, e).wait_send()
        for d in range(1, nm):
            mode_send(d, e).wait_send()
    for c in range(chunks):

        @pl.when(not_owner)
        def _():
            part_right(c).wait_send()

        @pl.when(jnp.logical_and(t <= owner, t > 0))
        def _():
            total_left(c).wait_send()

        @pl.when(jnp.logical_and(t >= owner, t < n - 1))
        def _():
            total_right(c).wait_send()


def local(n, nm, object_field, probe, offsets, counts, measured):
    f32 = jnp.float32
    tile, obj_c = object_field.shape[1:]
    nk, _, cut, frame = probe.shape
    slots = offsets.shape[1] // 2
    width = obj_c // (2 * nm)
    rows = tile + HALO
    chunks = 2 * nk
    dma = pltpu.SemaphoreType.DMA
    vmem = pl.BlockSpec(memory_space=pltpu.VMEM)
    hbm = pl.BlockSpec(memory_space=pl.ANY)
    peers = nm - 1
    tables = jnp.asarray(transform_tables(frame))
    picks = selectors(
        offsets, counts, lax.axis_index("scan") * tile, lax.axis_index("sub") * slots,
        slots, frame, tile, obj_c,
    )
    return pl.pallas_call(
        functools.partial(kernel, n, nm),
        out_shape=(
            jax.ShapeDtypeStruct((2, tile, width), f32),
            jax.ShapeDtypeStruct((nk, 2, cut, frame), f32),
        ),
        in_specs=[hbm, hbm, vmem, vmem, vmem, vmem, hbm, vmem],
        out_specs=(vmem, vmem),
        scratch_shapes=[
            pltpu.VMEM((2, rows, obj_c), f32),
            pltpu.VMEM((nk, 2, frame, frame), f32),
            pltpu.VMEM((slots, frame, frame), f32),
            pltpu.VMEM((slots, 2, frame, frame), f32),
            pltpu.VMEM((slots, nk, 2, frame, frame), f32),
            pltpu.VMEM((slots, frame, frame), f32),
            pltpu.VMEM((slots, peers, frame, frame), f32),
            pltpu.VMEM((slots, 2, frame, frame), f32),
            pltpu.VMEM((nk, 2, frame, frame), f32),
            pltpu.VMEM((nk, 2, cut, frame), f32),
            pltpu.VMEM((chunks, cut, frame), f32),
            pltpu.VMEM((chunks, cut, frame), f32),
            pltpu.VMEM((chunks, cut, frame), f32),
            pltpu.VMEM((chunks, cut, frame), f32),
            pltpu.VMEM((2, rows, obj_c), f32),
            pltpu.VMEM((nm, 2, rows, width), f32),
            pltpu.VMEM((nm, 2, rows, width), f32),
            pltpu.VMEM((peers, 2, rows, width), f32),
            pltpu.VMEM((2, HALO, width), f32),
            dma((3,)),
            dma((2,)),
            dma((2,)),
            dma((2, 2)),
            dma((2, 2)),
            dma((2, slots, peers)),
            dma((2, nk)),
            dma((chunks,)),
            dma((chunks,)),
            dma((chunks,)),
            dma((2, chunks)),
            dma((chunks,)),
            dma((2, nm, 2)),
            dma((2, peers, 2)),
            dma((2,)),
        ],
        compiler_params=pltpu.CompilerParams(
            collective_id=0, has_side_effects=True, vmem_limit_bytes=56 * 1024 * 1024
        ),
    )(object_field, probe, *picks, measured, tables)


def solution(mesh):
    in_specs = (
        P(None, ("groups", "scan"), None),
        P("mode", None, "sub", None),
        P(("groups", "scan"), None, None),
        P(("groups", "scan")),
        P(("groups", "scan"), None, None, "sub"),
    )
    out_specs = (
        P(None, ("groups", "scan"), ("mode", "sub")),
        P(("groups", "mode"), None, "sub", None),
    )
    body = functools.partial(local, mesh.shape["scan"], mesh.shape["mode"])
    return jax.shard_map(body, mesh=mesh, in_specs=in_specs, out_specs=out_specs, check_vma=False)
```

time: 327 us -> 98.8 us (0.30)
  waiting for transfers between devices: 135 us -> 0 us
  Pallas kernels: 0 us -> 88.8 us
  local copies, waits for them, and re-layouts: 76.2 us -> 4.99 us
  matrix products: 36.8 us -> 0 us
  blocking collectives: 19 us -> 0 us
  other arithmetic: 21.5 us -> 3.45 us
  loops' own time: 15.8 us -> 0 us
  between operations: 14.7 us -> 1.33 us
  starting transfers between devices: 4.74 us -> 0 us
    pallas_call x0 -> x1, Pallas kernels: none -> 88.8 us  [local(): pl.pallas_call(functools.partial(kernel, n, nm), out_shape=(jax.ShapeDtyp...]
    ppermute x2 -> x0, waiting for transfers between devices: 55.4 us -> none  [shifted(): return lax.ppermute(array, axis, pairs)]
    psum x2 -> x0, waiting for transfers between devices: 46.7 us -> none  [the longest x1 26.4 us: local(): intensity = lax.psum(energy, 'mode')]
    dot_general x4 -> x0, matrix products: 36.8 us -> none  [the longest x1 10.8 us: local(): jnp.einsum('abjr,mcarx->mcbjx', forward_table, column_pass, precision=hig...]
    reduce_scatter x1 -> x0, waiting for transfers between devices: 32.8 us -> none  [local(): lax.psum_scatter(own_rows, ('mode', 'sub'), scatter_dimension=2, tiled=True)]
    all_to_all x3 -> x0, local copies, waits for them, and re-layouts: 19 us -> none  [regroup(): lax.all_to_all(spectra, 'sub', split_axis=4, concat_axis=3, tiled=True)]
    all_to_all x2 -> x0, blocking collectives: 19 us -> none  [regroup(): lax.all_to_all(spectra, 'sub', split_axis=4, concat_axis=3, tiled=True)]
    dynamic_update_slice x4 -> x0, local copies, waits for them, and re-layouts: 16.1 us -> none  [add_slot(): lax.dynamic_update_slice(buffer, current + object_terms[slot_index], (jnp...]
  transfers between devices with their start and end apart: 5 -> 0, of which waited for: 5 -> 0; matrix products, arithmetic and copies ran while one was open for 5% -> 0% of each run, Pallas kernels for 0% -> 0%
where the time goes in v1:
time: 98.8 us; the launch traced here: 98.5 us
  Pallas kernels  88.8 us (90%)
  local copies, waits for them, and re-layouts  4.99 us (5%)
  other arithmetic  3.45 us (3%)
  between operations  1.33 us (1%)
    pallas_call x1, Pallas kernels, local(): pl.pallas_call(functools.partial(kernel, n, nm), out_shape=(jax.ShapeDtyp...  88.8 us
    unnamed x5, local copies, waits for them, and re-layouts  4.15 us

profile of v1, /device:TPU:24, one launch (start us, length us, event | category | flops | bytes accessed | tf_op | source)
XLA Modules:
  0.0 98.5 jit_solution(16867194004601398333)
XLA Ops:
  0.6 0.0 copy-start
  1.3 0.0 copy-done
  1.3 0.1 constant_dynamic-slice_fusion
  1.4 0.1 copy.9
  1.5 0.2 slice_reduce_fusion
  1.7 0.1 add_bitcast_fusion
  1.8 0.7 broadcast_in_dim.2.live
  2.4 0.1 iota_add_fusion
  2.5 0.8 fusion.2.put_rows
  3.3 0.9 fusion.1.take_rows
  4.2 1.4 %fusion.take_cols = bf16[1024,512]{1,0:T(8,128)(2,1)} fusion(s32[512]{0:T(512)S(1)} %bitcast.7), kind=kLoop, calls=%fused_computation.1 | loop fusion | flops 1048576 | bytes 1050624 | tf_op jit(solution)/shard_map/convert_element_type | solution.py:60
  5.6 88.8 %shard_map.77 = (f32[2,256,256]{2,1,0:T(8,128)}, f32[4,2,128,256]{3,2,1,0:T(8,128)}) custom-call(f32[2,256,1024]{2,1,0:T(8,128)} %obj.1, f32[4,2,128,256]{3,2,1,0:T(8,128)} %probe.1, bf16[2,256,384]{2,1,0:T(8,128)(2,1)} %fusion.1.take_rows, bf16[2,384,256]{2,1,0:T(8,128)(2,1)} %fusion.2.put_rows, bf16[1024,512]{1,0:T(8,128)(2,1)} %fusion.take_cols, ...), custom_call_target="tpu_custom_call" | custom-call | tf_op jit(solution)/shard_map/pallas_call | solution.py:472
  94.4 1.9 %copy.14 = f32[2,256,256]{2,1,0:T(8,128)} copy(f32[2,256,256]{2,1,0:T(8,128)} %get-tuple-element.6) | data formatting | bytes 1048576
  96.3 2.3 %copy.15 = f32[4,2,128,256]{3,2,1,0:T(8,128)} copy(f32[4,2,128,256]{3,2,1,0:T(8,128)} %get-tuple-element.7) | data formatting | bytes 2097152
  (2 shorter events, 0.0 us)
Async XLA Ops:
  0.6 0.7 copy-start

commit v2 on v1

--- a/solution.py
+++ b/solution.py
@@ -10,6 +10,8 @@
 from jax.sharding import PartitionSpec as P
 
 HALO = 128
+CUTS = 1
+UNROLL = 2
 MESH = pl.DeviceIdType.MESH
 
 
@@ -48,25 +50,26 @@
     return mm(a[0], b[0]) + (mm(a[1], b[0]) + mm(a[0], b[1]))
 
 
-def selectors(offsets, counts, tile_start, first, slots, frame, tile, obj_c):
+def selectors(offsets, counts, tile_start, first, slots, frame):
     own = lax.dynamic_slice_in_dim(offsets[0], first, slots, axis=0)
     pixel = jnp.arange(frame, dtype=jnp.int32)
-    row = (own[:, :1] - tile_start) + pixel
-    col = (own[:, 1:] + pixel).reshape(1, slots * frame)
-    rows = jnp.arange(tile + HALO, dtype=jnp.int32)
-    cols = jnp.arange(obj_c, dtype=jnp.int32)[:, None]
-    take_rows = (row[:, :, None] == rows[None, None, :]).astype(jnp.bfloat16)
-    put_rows = (rows[None, :, None] == row[:, None, :]).astype(jnp.bfloat16)
-    take_cols = (cols == col).astype(jnp.bfloat16)
-    live = (first + jnp.arange(slots, dtype=jnp.int32) < counts[0]).astype(jnp.float32)
-    return take_rows, put_rows, take_cols, jnp.broadcast_to(live[:, None, None], (slots, 1, frame))
+    length = slots * frame
+    col = (own[:, 1:] + pixel).reshape(1, length)
+    row = jnp.broadcast_to(own[:, :1] - tile_start, (slots, length))
+    slot = first + jnp.arange(slots, dtype=jnp.int32)
+    live = jnp.broadcast_to((slot < counts[0]).astype(jnp.int32)[:, None], (slots, length))
+    return jnp.concatenate([col, row, live])
+
+
+def ones_where(mask):
+    return jnp.where(mask, 1.0, 0.0).astype(jnp.bfloat16)
 
 
 def kernel(
-    n, nm, obj, probe, take_rows, put_rows, take_cols, live, meas, tabs, og, pg,
+    n, nm, obj, probe, sel, meas, tabs, og, pg,
     ext, pf, mf, q, spec, inten, inten_in, objt, pterm, px, x, p_left, p_right, tot,
-    g, g_in, h, h_in, hz,
-    loc_sem, probe_sem, meas_sem, halo_sem, fwd_sem, int_sem, px_sem, part_send, pl_sem, pr_sem,
+    g, g_in, h, h_in, hz, take_rows, put_rows, take_cols, picked,
+    loc_sem, probe_sem, meas_sem, halo_sem, across_sem, fwd_sem, int_sem, px_sem, part_send, pl_sem, pr_sem,
     tot_out, tot_in, gs_sem, hs_sem, hz_sem,
 ):
     t = lax.axis_index("scan")
@@ -81,9 +84,8 @@
     mcols = meas.shape[3]
     slots = mf.shape[0]
     width = og.shape[2]
-    half = obj_c // 2
     chunks = x.shape[0]
-    owner = (n - 1) // 2
+    near = n // 2 - 1
 
     def remote(src, dst, send, recv, **where):
         return pltpu.make_async_remote_copy(
@@ -121,17 +123,33 @@
         barrier, nm + (t > 0).astype(jnp.int32) + (t < n - 1).astype(jnp.int32)
     )
 
-    own_half = pl.ds(pl.multiple_of(sub * half, half), half)
+    def block(m, s):
+        return pl.ds(pl.multiple_of((m * 2 + s) * width, width), width)
 
     def halo(c):
         return remote(
-            obj.at[c, pl.ds(0, HALO), own_half], ext.at[c, pl.ds(tile, HALO), own_half],
+            obj.at[c, pl.ds(0, HALO), block(mode, sub)],
+            ext.at[c, pl.ds(tile, HALO), block(mode, sub)],
             halo_sem.at[0, c], halo_sem.at[1, c], scan=jnp.maximum(t - 1, 0),
         )
 
-    def forwarded(c):
-        part = ext.at[c, pl.ds(tile, HALO), own_half]
-        return remote(part, part, fwd_sem.at[0, c], fwd_sem.at[1, c], sub=sib)
+    def across(c, d):
+        part = ext.at[c, pl.ds(tile, HALO), block(mode, sub)]
+        return remote(
+            part, part, across_sem.at[0, c, d - 1], across_sem.at[1, c, d - 1],
+            mode=lax.rem(mode + d, nm),
+        )
+
+    def across_in(c, d):
+        part = ext.at[c, pl.ds(tile, HALO), block(lax.rem(mode + nm - d, nm), sub)]
+        return remote(
+            part, part, across_sem.at[0, c, d - 1], across_sem.at[1, c, d - 1],
+            mode=lax.rem(mode + d, nm),
+        )
+
+    def forwarded(c, d, s):
+        part = ext.at[c, pl.ds(tile, HALO), block(lax.rem(mode + nm - d, nm), s)]
+        return remote(part, part, fwd_sem.at[0, c, d], fwd_sem.at[1, c, d], sub=sib)
 
     @pl.when(t > 0)
     def _():
@@ -148,6 +166,27 @@
     )
     send_meas.start()
 
+    def iota(shape, axis):
+        return lax.broadcasted_iota(jnp.int32, shape, axis)
+
+    rows = tile + HALO
+    take_cols[...] = ones_where(iota((obj_c, slots * frame), 0) == sel[0:1])
+    for s in range(slots):
+        first = sel[1 + s : 2 + s]
+        take_rows[s] = ones_where(
+            iota((frame, rows), 1) - iota((frame, rows), 0) == first[:, :rows]
+        )
+        put_rows[s] = ones_where(
+            iota((rows, frame), 0) - iota((rows, frame), 1) == first[:, :frame]
+        )
+    own_obj.wait()
+
+    def pick(c, at, count):
+        high, low = split(ext[c, pl.ds(at, count)])
+        picked[c, pl.ds(at, count)] = mm(high, take_cols[...]) + mm(low, take_cols[...])
+
+    for c in range(2):
+        pick(c, 0, tile)
     objt[...] = jnp.zeros_like(objt)
     inten[...] = jnp.zeros_like(inten)
 
@@ -155,12 +194,19 @@
     def _():
         for c in range(2):
             halo(c).wait_recv()
-            forwarded(c).start()
+            for d in range(1, nm):
+                across(c, d).start()
+            forwarded(c, 0, sub).start()
         for c in range(2):
-            forwarded(c).wait_send()
-            forwarded(c).wait_recv()
-
-    own_obj.wait()
+            for d in range(1, nm):
+                across_in(c, d).wait_recv()
+                forwarded(c, d, sub).start()
+        for c in range(2):
+            for d in range(nm):
+                forwarded(c, d, sib).wait_recv()
+                forwarded(c, d, sub).wait_send()
+            for d in range(1, nm):
+                across(c, d).wait_send()
 
     @pl.when(t == n - 1)
     def _():
@@ -170,10 +216,9 @@
     send_probe.wait()
 
     for c in range(2):
-        high, low = split(ext[c])
-        picked = mm(high, take_cols[...]) + mm(low, take_cols[...])
+        pick(c, tile, HALO)
         for s in range(slots):
-            high, low = split(picked[:, s * frame : (s + 1) * frame])
+            high, low = split(picked[c, :, s * frame : (s + 1) * frame])
             q[s, c] = mm(take_rows[s], high) + mm(take_rows[s], low)
 
     def table(i):
@@ -205,7 +250,7 @@
             inten[s] += zr * zr + zi * zi
             return carry
 
-        lax.fori_loop(0, nk, forward, 0)
+        lax.fori_loop(0, nk, forward, 0, unroll=UNROLL)
         for d in range(1, nm):
             send_inten(s, d).start()
 
@@ -217,9 +262,11 @@
             pterm.at[k, :, sib_rows], px.at[k], px_sem.at[0, k], px_sem.at[1, k], sub=sib
         )
 
-    not_owner = t != owner
+    middle = jnp.logical_or(t == near, t == near + 1)
     has_outer = jnp.logical_and(t > 0, t < n - 1)
-    below = t < owner
+    below = t <= near
+    send_total_left = jnp.logical_and(below, t > 0)
+    send_total_right = jnp.logical_and(t > near, t < n - 1)
 
     def part_right(c):
         return remote(
@@ -246,19 +293,22 @@
         def _():
             part_right(c).start()
 
-        @pl.when(t > owner)
+        @pl.when(t > near)
         def _():
             part_left(c).start()
 
     def ready(k):
         px_copy(k).wait_recv()
         for c in range(2):
-            x[2 * k + c] = pterm[k, c, own_rows] + px[k, c]
-
-        @pl.when(jnp.logical_and(not_owner, jnp.logical_not(has_outer)))
-        def _():
-            for c in range(2):
-                send_part(2 * k + c)
+            for i in range(CUTS):
+                at = i * (cut // CUTS)
+                part = pl.ds(pl.multiple_of(sub * cut + at, cut // CUTS), cut // CUTS)
+                x[(2 * k + c) * CUTS + i] = pterm[k, c, part] + px[k, c, pl.ds(at, cut // CUTS)]
+
+        @pl.when(jnp.logical_not(has_outer))
+        def _():
+            for c in range(2 * CUTS):
+                send_part(2 * CUTS * k + c)
 
     for s in range(slots):
         for d in range(1, nm):
@@ -266,7 +316,8 @@
         total = inten[s]
         for d in range(1, nm):
             total = total + inten_in[s, d - 1]
-        inten_in[s, 0] = live[s] * (1.0 - jnp.sqrt(mf[s] + 1.0) * lax.rsqrt(total + 1.0))
+        live = sel[1 + slots + s : 2 + slots + s, :frame].astype(jnp.float32)
+        inten_in[s, 0] = live * (1.0 - jnp.sqrt(mf[s] + 1.0) * lax.rsqrt(total + 1.0))
 
         def backward(k, carry):
             scale = inten_in[s, 0]
@@ -293,7 +344,7 @@
 
             return carry
 
-        lax.fori_loop(0, nk, backward, 0)
+        lax.fori_loop(0, nk, backward, 0, unroll=UNROLL)
 
     ready(nk - 1)
 
@@ -307,9 +358,6 @@
 
     spans = (pl.ds(tile, HALO), pl.ds(0, tile))
 
-    def block(m, s):
-        return pl.ds(pl.multiple_of((m * 2 + s) * width, width), width)
-
     def sib_send(m, e):
         return remote(
             g.at[:, spans[e], block(m, sib)], g_in.at[m, :, spans[e]],
@@ -327,18 +375,20 @@
         h.at[mode, :, spans[0]], hz, hz_sem.at[0], hz_sem.at[1], scan=jnp.minimum(t + 1, n - 1)
     )
 
+    order = [lax.rem(mode + d, nm) for d in range(1, nm)] + [mode]
+
     def start_sib():
-        for e in range(2):
-            for m in range(nm):
+        for m in order:
+            for e in range(2):
                 sib_send(m, e).start()
 
     def sum_sib():
-        for e in range(2):
-            for m in range(nm):
+        for d, m in enumerate(order, 1):
+            for e in range(2):
                 sib_send(m, e).wait_recv()
                 h[m, :, spans[e]] = g[:, spans[e], block(m, sub)] + g_in[m, :, spans[e]]
-            for d in range(1, nm):
-                mode_send(d, e).start()
+                if d < nm:
+                    mode_send(d, e).start()
 
     def sum_mode(e):
         for d in range(1, nm):
@@ -356,60 +406,56 @@
             og[...] = whole
 
     def inward(c):
-        @pl.when(jnp.logical_and(not_owner, has_outer))
+        @pl.when(has_outer)
         def _():
             @pl.when(below)
             def _():
                 part_right(c).wait_recv()
                 x[c] += p_left[c]
 
-            @pl.when(t > owner)
+            @pl.when(t > near)
             def _():
                 part_left(c).wait_recv()
                 x[c] += p_right[c]
 
             send_part(c)
 
-        @pl.when(t == owner)
-        def _():
-            if owner > 0:
-                part_right(c).wait_recv()
-                x[c] += p_left[c]
-            if owner < n - 1:
-                part_left(c).wait_recv()
-                x[c] += p_right[c]
-            tot[c] = x[c] * (1.0 / n)
-            if owner > 0:
-                total_left(c).start()
-            if owner < n - 1:
-                total_right(c).start()
-            pg[c // 2, c % 2] = tot[c]
-
-    def outward(c):
-        @pl.when(not_owner)
+    def finish(c):
+        @pl.when(t == near)
+        def _():
+            part_left(c).wait_recv()
+            tot[c] = (x[c] + p_right[c]) * (1.0 / n)
+
+        @pl.when(t == near + 1)
+        def _():
+            part_right(c).wait_recv()
+            tot[c] = (x[c] + p_left[c]) * (1.0 / n)
+
+        @pl.when(jnp.logical_not(middle))
         def _():
             total_left(c).wait_recv()
 
-            @pl.when(jnp.logical_and(below, t > 0))
-            def _():
-                total_left(c).start()
-
-            @pl.when(jnp.logical_and(t > owner, t < n - 1))
-            def _():
-                total_right(c).start()
-
-            pg[c // 2, c % 2] = tot[c]
+        @pl.when(send_total_left)
+        def _():
+            total_left(c).start()
+
+        @pl.when(send_total_right)
+        def _():
+            total_right(c).start()
+
+        at = c % CUTS * (cut // CUTS)
+        pg[c // (2 * CUTS), c // CUTS % 2, pl.ds(at, cut // CUTS)] = tot[c]
 
     start_sib()
     inward(0)
+    inward(1)
     sum_sib()
     lag = 2
-    for c in range(1, chunks + lag):
+    for c in range(2, chunks + lag):
         if c < chunks:
             inward(c)
-        if c >= lag:
-            outward(c - lag)
-        if c == chunks // 2:
+        finish(c - lag)
+        if c == max(2, chunks // 2):
             sum_mode(0)
     sum_mode(1)
 
@@ -439,15 +485,13 @@
             mode_send(d, e).wait_send()
     for c in range(chunks):
 
-        @pl.when(not_owner)
-        def _():
-            part_right(c).wait_send()
-
-        @pl.when(jnp.logical_and(t <= owner, t > 0))
+        part_right(c).wait_send()
+
+        @pl.when(send_total_left)
         def _():
             total_left(c).wait_send()
 
-        @pl.when(jnp.logical_and(t >= owner, t < n - 1))
+        @pl.when(send_total_right)
         def _():
             total_right(c).wait_send()
 
@@ -459,7 +503,7 @@
     slots = offsets.shape[1] // 2
     width = obj_c // (2 * nm)
     rows = tile + HALO
-    chunks = 2 * nk
+    chunks = 2 * nk * CUTS
     dma = pltpu.SemaphoreType.DMA
     vmem = pl.BlockSpec(memory_space=pltpu.VMEM)
     hbm = pl.BlockSpec(memory_space=pl.ANY)
@@ -467,7 +511,7 @@
     tables = jnp.asarray(transform_tables(frame))
     picks = selectors(
         offsets, counts, lax.axis_index("scan") * tile, lax.axis_index("sub") * slots,
-        slots, frame, tile, obj_c,
+        slots, frame,
     )
     return pl.pallas_call(
         functools.partial(kernel, n, nm),
@@ -475,7 +519,7 @@
             jax.ShapeDtypeStruct((2, tile, width), f32),
             jax.ShapeDtypeStruct((nk, 2, cut, frame), f32),
         ),
-        in_specs=[hbm, hbm, vmem, vmem, vmem, vmem, hbm, vmem],
+        in_specs=[hbm, hbm, vmem, hbm, vmem],
         out_specs=(vmem, vmem),
         scratch_shapes=[
             pltpu.VMEM((2, rows, obj_c), f32),
@@ -488,20 +532,25 @@
             pltpu.VMEM((slots, 2, frame, frame), f32),
             pltpu.VMEM((nk, 2, frame, frame), f32),
             pltpu.VMEM((nk, 2, cut, frame), f32),
-            pltpu.VMEM((chunks, cut, frame), f32),
-            pltpu.VMEM((chunks, cut, frame), f32),
-            pltpu.VMEM((chunks, cut, frame), f32),
-            pltpu.VMEM((chunks, cut, frame), f32),
+            pltpu.VMEM((chunks, cut // CUTS, frame), f32),
+            pltpu.VMEM((chunks, cut // CUTS, frame), f32),
+            pltpu.VMEM((chunks, cut // CUTS, frame), f32),
+            pltpu.VMEM((chunks, cut // CUTS, frame), f32),
             pltpu.VMEM((2, rows, obj_c), f32),
             pltpu.VMEM((nm, 2, rows, width), f32),
             pltpu.VMEM((nm, 2, rows, width), f32),
             pltpu.VMEM((peers, 2, rows, width), f32),
             pltpu.VMEM((2, HALO, width), f32),
+            pltpu.VMEM((slots, frame, rows), jnp.bfloat16),
+            pltpu.VMEM((slots, rows, frame), jnp.bfloat16),
+            pltpu.VMEM((obj_c, slots * frame), jnp.bfloat16),
+            pltpu.VMEM((2, rows, slots * frame), f32),
             dma((3,)),
             dma((2,)),
             dma((2,)),
             dma((2, 2)),
-            dma((2, 2)),
+            dma((2, 2, peers)),
+            dma((2, 2, nm)),
             dma((2, slots, peers)),
             dma((2, nk)),
             dma((chunks,)),
@@ -516,7 +565,7 @@
         compiler_params=pltpu.CompilerParams(
             collective_id=0, has_side_effects=True, vmem_limit_bytes=56 * 1024 * 1024
         ),
-    )(object_field, probe, *picks, measured, tables)
+    )(object_field, probe, picks, measured, tables)
 
 
 def solution(mesh):

time: 98.8 us -> 86.8 us (0.88)
  Pallas kernels: 88.8 us -> 79.8 us
  other arithmetic: 3.45 us -> 0.94 us
    pallas_call x1, Pallas kernels: 88.8 us -> 79.8 us  [local(): pl.pallas_call(functools.partial(kernel, n, nm), out_shape=(jax.ShapeDtyp...]
    convert_element_type x4 -> x1, other arithmetic: 3.12 us -> 0.01 us  [selectors(): (slot < counts[0]).astype(jnp.int32)[:, None]]
where the time goes in v2:
time: 86.8 us; the launch traced here: 86.6 us
  Pallas kernels  79.8 us (92%)
  local copies, waits for them, and re-layouts  4.47 us (5%)
  between operations  1.32 us (2%)
  other arithmetic  0.94 us (1%)
    pallas_call x1, Pallas kernels, local(): pl.pallas_call(functools.partial(kernel, n, nm), out_shape=(jax.ShapeDtyp...  79.8 us
    unnamed x5, local copies, waits for them, and re-layouts  4.15 us

profile of v2, /device:TPU:24, one launch (start us, length us, event | category | flops | bytes accessed | tf_op | source)
XLA Modules:
  0.0 86.6 jit_solution(966537638684930213)
XLA Ops:
  0.6 0.0 copy-start
  1.3 0.1 pad.2.clone
  1.4 0.0 copy-done
  1.4 0.1 constant_dynamic-slice_fusion
  1.5 0.1 copy.9
  1.6 0.2 subtract_reduce_fusion
  1.7 0.1 pad.1.clone
  1.8 0.1 add_bitcast_fusion
  1.9 0.7 add_add_fusion.sel
  2.6 79.8 %shard_map.77 = (f32[2,256,256]{2,1,0:T(8,128)}, f32[4,2,128,256]{3,2,1,0:T(8,128)}) custom-call(f32[2,256,1024]{2,1,0:T(8,128)} %obj.1, f32[4,2,128,256]{3,2,1,0:T(8,128)} %probe.1, s32[5,512]{1,0:T(8,128)} %add_add_fusion.sel, f32[1,4,256,128]{3,2,1,0:T(8,128)} %meas.1, bf16[6,256,256]{2,1,0:T(8,128)(2,1)} %constant.20.clone.tabs), custom_call_target="tpu_custom_call" | custom-call | tf_op jit(solution)/shard_map/pallas_call | solution.py:516
  82.4 1.9 %copy.14 = f32[2,256,256]{2,1,0:T(8,128)} copy(f32[2,256,256]{2,1,0:T(8,128)} %get-tuple-element.6) | data formatting | bytes 1048576
  84.3 2.3 %copy.15 = f32[4,2,128,256]{3,2,1,0:T(8,128)} copy(f32[4,2,128,256]{3,2,1,0:T(8,128)} %get-tuple-element.7) | data formatting | bytes 2097152
  (2 shorter events, 0.0 us)
Async XLA Ops:
  0.6 0.8 copy-start
